TPU v7x, 32 devices: a whole 2x2x4 slice. The times are simulated.
32 devices in a mesh: batch: 4 (over z), pos: 8 (over y, x, core).
Axes of the slice: x: 2, y: 2, z: 4, core: 2. Of those that a mesh axis runs over, the one named last changes fastest.
Arguments:
- inputs: bfloat16 [4, 4096, 1536], P('batch', 'pos'), may hold values from -6 to 6
- bn_scale: float32 [1536], replicated, may hold values from 0.25 to 1.75
- bn_shift: float32 [1536], replicated, may hold values from -2 to 2
- mid_scale: float32 [384], replicated, may hold values from 0.25 to 1.75
- mid_shift: float32 [384], replicated, may hold values from -2 to 2
- dilated_weight: bfloat16 [1536, 3, 384], P('batch'), may hold values from -0.09375 to 0.09375
- w_point: bfloat16 [384, 1536], P('batch'), may hold values from -0.3125 to 0.3125
- head: bfloat16 [5120, 1536], P('pos'), may hold values from -0.15625 to 0.15625
- targets: bfloat16 [4, 4096, 512], P('batch', 'pos'), may hold values from 0 to 2
- assay_slots: int32 [4, 512], P('batch', 'pos'), may hold values from 0 to 639, as said below
- assay_counts: int32 [4, 8], P('batch', 'pos'), may hold values from 1 to 64, as said below
Outputs:
- d_inputs: bfloat16 [4, 4096, 1536], P('batch', 'pos')
- new_head: bfloat16 [5120, 1536], P('pos')
Inputs may be any that keep to these rules, and one draw needn't show every extreme that they name: `assay_slots`: within each block of 64 slots (one shard of one sequence) the entries are distinct. `assay_counts`: in every sequence some shard has all 64 slots live.
All inputs are finite; a program needn't handle non-finite values.
Results may differ from a plain program's by a relative error of at most 0.012.
Values may be sent and summed in bfloat16 or wider, within the bound.
A program may use at most 64 MiB of HBM per device.

v0:
```python
import jax
import jax.numpy as jnp
from jax import lax
from jax.sharding import PartitionSpec as P

DILATION_STEP = 32


def with_halo(shard, sides, width):
    for axis, dim in sides:
        peers, length = (lax.axis_size(axis), shard.shape[dim])
        up = [(i, (i + 1) % peers) for i in range(peers - 1)]
        down = [(j, i) for i, j in up]
        last = lax.slice_in_dim(shard, length - width, length, axis=dim)
        initial = lax.slice_in_dim(shard, 0, width, axis=dim)
        before = lax.ppermute(last, axis, up)
        after = lax.ppermute(initial, axis, down)
        shard = jnp.concatenate([before, shard, after], axis=dim)
    return shard


def gelu_slope(value):
    return jax.jvp(jax.nn.gelu, (value,), (jnp.ones_like(value),))[1]


def per_device(
    inputs,
    bn_scale,
    bn_shift,
    mid_scale,
    mid_shift,
    dilated_weight,
    w_point,
    head,
    targets,
    assay_slots,
    assay_counts,
):
    contract = (((1,), (1,)), ((), ()))
    kernel, pointwise = (
        lax.all_gather(dilated_weight, "batch", axis=0, tiled=True),
        lax.all_gather(w_point, "batch", axis=0, tiled=True),
    )
    stream = inputs[0]
    rows = stream.shape[0]
    window_length = DILATION_STEP
    first = stream.astype(jnp.float32) * bn_scale + bn_shift
    acted = jax.nn.gelu(first).astype(jnp.bfloat16)
    padded_input = with_halo(acted, (("pos", 0),), window_length)
    hidden_state = jnp.dot(
        padded_input[0:rows], kernel[:, 0, :], preferred_element_type=jnp.float32
    )
    hidden_state = hidden_state + jnp.dot(
        padded_input[window_length : window_length + rows],
        kernel[:, 1, :],
        preferred_element_type=jnp.float32,
    )
    hidden_state = hidden_state + jnp.dot(
        padded_input[2 * window_length : 2 * window_length + rows],
        kernel[:, 2, :],
        preferred_element_type=jnp.float32,
    )
    second = hidden_state * mid_scale + mid_shift
    mid = jax.nn.gelu(second).astype(jnp.bfloat16)
    embed = (
        stream.astype(jnp.float32) + jnp.dot(mid, pointwise, preferred_element_type=jnp.float32)
    ).astype(jnp.bfloat16)
    slots = assay_slots[0]
    slot_count = slots.shape[0]
    chosen = head[slots]
    live_mark = (jnp.arange(slot_count) < assay_counts[0, 0]).astype(jnp.bfloat16)
    selected, live_all = (
        lax.all_gather(chosen, "pos", axis=0, tiled=True),
        lax.all_gather(live_mark, "pos", axis=0, tiled=True),
    )
    pre = lax.dot_general(embed, selected, contract, preferred_element_type=jnp.float32)
    goal = targets[0].astype(jnp.float32)
    delta = (
        live_all.astype(jnp.float32) * (jax.nn.softplus(pre) - goal) * jax.nn.sigmoid(pre)
    ).astype(jnp.bfloat16)
    back = jnp.dot(delta, selected, preferred_element_type=jnp.float32).astype(jnp.bfloat16)
    dmid = lax.dot_general(back, pointwise, contract, preferred_element_type=jnp.float32)
    dhid = (dmid * gelu_slope(second) * mid_scale).astype(jnp.bfloat16)
    padded_grad = with_halo(dhid, (("pos", 0),), window_length)
    dact = lax.dot_general(
        padded_grad[2 * window_length : 2 * window_length + rows],
        kernel[:, 0, :],
        contract,
        preferred_element_type=jnp.float32,
    )
    dact = dact + lax.dot_general(
        padded_grad[window_length : window_length + rows],
        kernel[:, 1, :],
        contract,
        preferred_element_type=jnp.float32,
    )
    dact = dact + lax.dot_general(
        padded_grad[0:rows], kernel[:, 2, :], contract, preferred_element_type=jnp.float32
    )
    d_inputs = (back.astype(jnp.float32) + dact * gelu_slope(first) * bn_scale).astype(jnp.bfloat16)
    owned = lax.psum_scatter(
        lax.dot_general(
            delta, embed, (((0,), (0,)), ((), ())), preferred_element_type=jnp.float32
        ).astype(jnp.bfloat16),
        "pos",
        scatter_dimension=0,
        tiled=True,
    ).astype(jnp.float32)
    spread = jnp.zeros((head.shape[0], owned.shape[1]), jnp.float32).at[slots].add(owned)
    d_head = lax.psum(spread.astype(jnp.bfloat16), "batch").astype(jnp.float32)
    new_head = (head.astype(jnp.float32) - 0.004 * d_head).astype(jnp.bfloat16)
    return (d_inputs[None], new_head)


def solution(mesh):
    in_specs = (
        P("batch", "pos", None),
        P(),
        P(),
        P(),
        P(),
        P("batch", None, None),
        P("batch", None),
        P("pos", None),
        P("batch", "pos", None),
        P("batch", "pos"),
        P("batch", "pos"),
    )
    out_specs = (P("batch", "pos", None), P("pos", None))
    return jax.shard_map(
        per_device, mesh=mesh, in_specs=in_specs, out_specs=out_specs, check_vma=False
    )
```

profile of v0, /device:TPU:0, one launch (start us, length us, event | category | flops | bytes accessed | tf_op | source)
XLA Modules:
  0.0 286.1 jit_solution(2264082619135657359)
XLA Ops:
  7.3 0.7 all-gather.5.cloned.1.call-update
  8.0 0.7 all-gather.7.cloned.1.call-update
  8.7 0.7 fusion.71
  9.4 3.4 %gather_fusion = bf16[64,1536]{1,0:T(8,128)(2,1)} fusion(bf16[640,1536]{1,0:T(8,128)(2,1)} %param.18, s32[1024]{0:T(1024)S(1)} %pad_clamp_fusion), kind=kCustom, calls=%fused_computation | custom fusion | bytes 393472 | tf_op jit(solution)/shard_map/gather | solution.py:70
  12.9 1.3 fusion.12
  14.2 2.4 collective-permute-start
  16.6 1.3 collective-permute-start.1
  18.5 0.6 dynamic-slice
  19.9 17.5 %all-reduce = bf16[512]{0:T(512)(128)(2,1)S(1)} all-reduce(bf16[512]{0:T(512)(128)(2,1)S(1)} %dynamic-update-slice), channel_id=1, replica_groups=mesh['batch'=4,'pos'=8] {'pos'}, use_global_device_ids=true, to_apply=%add | all-reduce | flops 512 | bytes 2048
  37.4 44.9 %all-gather.5.cloned.1.call-done = bf16[1536,3,384]{2,0,1:T(8,128)(2,1)} async-done(((bf16[384,3,384]{2,0,1:T(8,128)(2,1)}), bf16[1536,3,384]{2,0,1:T(8,128)(2,1)}) %all-gather.5.cloned.1.call-update) | async-done | bytes 3538960 | tf_op jit(solution)/shard_map/all_gather | solution.py:41
  82.3 2.8 fusion.38
  85.2 1.9 fusion.34
  87.1 1.9 fusion.44
  89.0 23.9 %all-gather.7.cloned.1.call-done = bf16[384,1536]{1,0:T(8,128)(2,1)} async-done(((bf16[96,1536]{1,0:T(8,128)(2,1)}), bf16[384,1536]{1,0:T(8,128)(2,1)}) %all-gather.7.cloned.1.call-update) | async-done | bytes 1179664 | tf_op jit(solution)/shard_map/all_gather | solution.py:42
  113.0 2.5 fusion.29
  115.5 24.8 %all-gather.9.cloned.1.call-done = bf16[512,1536]{1,0:T(8,128)(2,1)} async-done(((bf16[64,1536]{1,0:T(8,128)(2,1)}), bf16[512,1536]{1,0:T(8,128)(2,1)}) %all-gather.9.cloned.1.call-update) | async-done | bytes 1572880 | tf_op jit(solution)/shard_map/all_gather | solution.py:73
  140.3 2.5 fusion.90
  142.8 1.0 copy-done.13
  143.7 4.3 %convolution_convert_fusion = bf16[512,1536]{1,0:T(8,128)(2,1)} fusion(bf16[512,1536]{1,0:T(8,128)(2,1)} %copy-done.12, f32[512,512]{1,0:T(8,128)S(1)} %fusion.90, bf16[1,512,512]{2,1,0:T(8,128)(2,1)S(1)} %copy-done.8, f32[512]{0:T(512)S(1)} %convert_element_type.70), kind=kOutput, calls=%fused_computation.39 | convolution fusion | flops 809762816 | bytes 4720640 | tf_op jit(solution)/shard_map/dot_general | solution.py:102
  148.2 4.1 %convolution_convert_fusion.1 = bf16[512,1536]{1,0:T(8,128)(2,1)} fusion(bf16[512,1536]{1,0:T(8,128)(2,1)S(1)} %copy-done.6, f32[512,512]{1,0:T(8,128)} %copy-done.13, bf16[1,512,512]{2,1,0:T(8,128)(2,1)} %param.19, f32[512]{0:T(512)S(1)} %convert_element_type.70), kind=kOutput, calls=%fused_computation.40 | convolution fusion | flops 809762816 | bytes 4720640 | tf_op jit(solution)/shard_map/dot_general | solution.py:81
  152.2 34.5 %reduce-scatter.2.cloned.1.call-done = bf16[64,1536]{1,0:T(8,128)(2,1)} async-done(((bf16[512,1536]{1,0:T(8,128)(2,1)}), bf16[64,1536]{1,0:T(8,128)(2,1)}) %reduce-scatter.2.cloned.1.call-update) | async-done | bytes 196624 | tf_op jit(solution)/shard_map/reduce_scatter | solution.py:101
  186.7 3.7 %scatter_custom_fusion = f32[640,1536]{1,0:T(8,128)} fusion(s32[64]{0:T(128)S(1)} %fusion.71, f32[]{:T(128)} %constant.15.clone.1, bf16[64,1536]{1,0:T(8,128)(2,1)} %reduce-scatter.2.cloned.1.call-done), kind=kCustom, calls=%fused_computation.43 | custom fusion | flops 196608 | bytes 4128772 | tf_op jit(solution)/shard_map/scatter-add | solution.py:109
  190.4 3.7 %convert_element_type.89 = bf16[640,1536]{1,0:T(8,128)(2,1)} convert(f32[640,1536]{1,0:T(8,128)} %scatter_custom_fusion) | non-fusion elementwise | flops 983040 | bytes 5898240 | tf_op jit(solution)/shard_map/convert_element_type | solution.py:110
  194.1 3.0 %fusion.45 = bf16[512,384]{1,0:T(8,128)(2,1)S(1)} fusion(bf16[512,1536]{1,0:T(8,128)(2,1)} %convolution_convert_fusion.1, bf16[384,1536]{1,0:T(8,128)(2,1)S(1)} %copy-done.7, f32[512,384]{1,0:T(8,128)} %fusion.44, f32[384]{0:T(512)S(1)} %copy-done.10), kind=kOutput, calls=%fused_computation.59 | convolution fusion | flops 607715328 | bytes 3933696 | tf_op jit(solution)/shard_map/dot_general | solution.py:82
  197.2 1.3 collective-permute-start.2
  198.5 3.0 %collective-permute-start.3 = (bf16[32,384]{1,0:T(8,128)(2,1)S(1)}, bf16[32,384]{1,0:T(8,128)(2,1)S(1)}, u32[]{:S(2)}, u32[]{:S(2)}) collective-permute-start(bf16[32,384]{1,0:T(8,128)(2,1)S(1)} %get-tuple-element.5), channel_id=1, source_target_pairs={{0,1},{1,2},{2,3},{3,4},{4,5},{5,6},{6,7},{8,9},{9,10},{10,11},{11... | collective-permute-start | bytes 73736 | tf_op jit(solution)/shard_map/ppermute | solution.py:16
  201.5 1.0 fusion.50
  202.6 1.0 fusion.51
  203.6 0.3 copy-done.14
  204.0 4.0 %fusion.30 = bf16[1,512,1536]{2,1,0:T(8,128)(2,1)} fusion(bf16[1,512,1536]{2,1,0:T(8,128)(2,1)S(1)} %copy-done.1, f32[512,1536]{1,0:T(8,128)S(1)} %fusion.51, f32[512,1536]{1,0:T(8,128)S(1)} %fusion.50, bf16[512,1536]{1,0:T(8,128)(2,1)S(1)} %copy-done.14, f32[1536]{0:T(1024)S(1)} %copy-done.4, f32[1536]{0:T(1024)S(1)} %copy-done.5, ...), kind=kOutput, calls=%fused_computation.42 | convolution fusion | flops 625213440 | bytes 12623872 | tf_op jit(solution)/shard_map/dot_general | solution.py:85
  207.9 68.3 %all-reduce.3.cloned.1.call-done = bf16[640,1536]{1,0:T(8,128)(2,1)} async-done(((bf16[640,1536]{1,0:T(8,128)(2,1)}), bf16[640,1536]{1,0:T(8,128)(2,1)}) %all-reduce.3.cloned.1.call-update) | async-done | bytes 1966096 | tf_op jit(solution)/shard_map/psum | solution.py:110
  276.2 3.4 %subtract_convert_fusion = bf16[640,1536]{1,0:T(8,128)(2,1)} fusion(bf16[640,1536]{1,0:T(8,128)(2,1)} %all-reduce.3.cloned.1.call-done, bf16[640,1536]{1,0:T(8,128)(2,1)S(1)} %copy-done), kind=kLoop, calls=%fused_computation.9 | loop fusion | flops 4915200 | bytes 5898240 | tf_op jit(solution)/shard_map/convert_element_type | solution.py:111
  (47 shorter events, 0.6 us)
Async XLA Ops:
  7.2 11.4 %copy-start.11 = (u32[32]{0:T(128)S(1)}, u32[32]{0:T(128)}, u32[]{:S(2)}) copy-start(u32[32]{0:T(128)} %constant.34) | copy-start | bytes 388
  7.2 5.7 %copy-start.1 = (bf16[1,512,1536]{2,1,0:T(8,128)(2,1)S(1)}, bf16[1,512,1536]{2,1,0:T(8,128)(2,1)}, u32[]{:S(2)}) copy-start(bf16[1,512,1536]{2,1,0:T(8,128)(2,1)} %param.11) | copy-start | bytes 4718596
  7.2 5.7 %copy-start.4 = (f32[1536]{0:T(1024)S(1)}, f32[1536]{0:T(1024)}, u32[]{:S(2)}) copy-start(f32[1536]{0:T(1024)} %param.13) | copy-start | bytes 18436
  7.2 5.7 %copy-start.5 = (f32[1536]{0:T(1024)S(1)}, f32[1536]{0:T(1024)}, u32[]{:S(2)}) copy-start(f32[1536]{0:T(1024)} %param.12) | copy-start | bytes 18436
  7.2 75.1 %all-gather.5.cloned.1.call-start = ((), (), s32[]{:S(2)}) async-start(), calls=%async_computation.1 | async-start | bytes 4423680 | tf_op jit(solution)/shard_map/all_gather | solution.py:41
  7.9 105.0 %all-gather.7.cloned.1.call-start = ((), (), s32[]{:S(2)}) async-start(), calls=%async_computation.2 | async-start | bytes 1474560 | tf_op jit(solution)/shard_map/all_gather | solution.py:42
  8.7 131.6 %all-gather.9.cloned.1.call-start = ((), (), s32[]{:S(2)}) async-start(), calls=%async_computation.5 | async-start | bytes 1769472 | tf_op jit(solution)/shard_map/all_gather | solution.py:73
  12.8 173.9 %reduce-scatter.2.cloned.1.call-start = ((), (), s32[]{:S(2)}) async-start(), calls=%async_computation.3 | async-start | bytes 1769472 | tf_op jit(solution)/shard_map/reduce_scatter | solution.py:101
  14.2 72.9 %collective-permute-start = (bf16[32,1536]{1,0:T(8,128)(2,1)S(1)}, bf16[32,1536]{1,0:T(8,128)(2,1)S(1)}, u32[]{:S(2)}, u32[]{:S(2)}) collective-permute-start(bf16[32,1536]{1,0:T(8,128)(2,1)S(1)} %get-tuple-element.2), channel_id=1, source_target_pairs={{0,1},{1,2},{2,3},{3,4},{4,5},{5,6},{6,7},{8,9},{9,10},{10,11},{11... | collective-permute-start | bytes 294920 | tf_op jit(solution)/shard_map/ppermute | solution.py:16
  16.6 68.6 %collective-permute-start.1 = (bf16[32,1536]{1,0:T(8,128)(2,1)S(1)}, bf16[32,1536]{1,0:T(8,128)(2,1)}, u32[]{:S(2)}, u32[]{:S(2)}) collective-permute-start(bf16[32,1536]{1,0:T(8,128)(2,1)S(1)} %get-tuple-element.3), channel_id=1, source_target_pairs={{1,0},{2,1},{3,2},{4,3},{5,4},{6,5},{7,6},{9,8},{10,9},{11,10},{12... | collective-permute-start | bytes 294920 | tf_op jit(solution)/shard_map/ppermute | solution.py:17
  82.3 2.9 %copy-start.2 = (bf16[1536,3,384]{2,0,1:T(8,128)(2,1)S(1)}, bf16[1536,3,384]{2,0,1:T(8,128)(2,1)}, u32[]{:S(2)}) copy-start(bf16[1536,3,384]{2,0,1:T(8,128)(2,1)} %all-gather.5.cloned.1.call-done) | copy-start | bytes 10616836
  85.1 1.9 copy-start.9
  85.2 1.9 copy-start.10
  115.5 24.8 %copy-start.12 = (bf16[512,1536]{1,0:T(8,128)(2,1)}, bf16[512,1536]{1,0:T(8,128)(2,1)S(1)}, u32[]{:S(2)}) copy-start(bf16[512,1536]{1,0:T(8,128)(2,1)S(1)} %fusion.29) | copy-start | bytes 4718596
  140.3 3.5 %copy-start.8 = (bf16[1,512,512]{2,1,0:T(8,128)(2,1)S(1)}, bf16[1,512,512]{2,1,0:T(8,128)(2,1)}, u32[]{:S(2)}) copy-start(bf16[1,512,512]{2,1,0:T(8,128)(2,1)} %param.19) | copy-start | bytes 1572868
  142.8 1.0 copy-start.13
  143.7 4.4 %copy-start.6 = (bf16[512,1536]{1,0:T(8,128)(2,1)S(1)}, bf16[512,1536]{1,0:T(8,128)(2,1)}, u32[]{:S(2)}) copy-start(bf16[512,1536]{1,0:T(8,128)(2,1)} %all-gather.9.cloned.1.call-done) | copy-start | bytes 4718596
  148.1 128.1 %all-reduce.3.cloned.1.call-start = ((), (), s32[]{:S(2)}) async-start(), calls=%async_computation.4 | async-start | bytes 3932160 | tf_op jit(solution)/shard_map/psum | solution.py:110
  190.4 3.7 %copy-start.7 = (bf16[384,1536]{1,0:T(8,128)(2,1)S(1)}, bf16[384,1536]{1,0:T(8,128)(2,1)}, u32[]{:S(2)}) copy-start(bf16[384,1536]{1,0:T(8,128)(2,1)} %all-gather.7.cloned.1.call-done) | copy-start | bytes 3538948
  194.1 7.4 %copy-start.3 = (bf16[1536,3,384]{2,0,1:T(8,128)(2,1)S(1)}, bf16[1536,3,384]{2,0,1:T(8,128)(2,1)}, u32[]{:S(2)}) copy-start(bf16[1536,3,384]{2,0,1:T(8,128)(2,1)} %all-gather.5.cloned.1.call-done) | copy-start | bytes 10616836
  197.2 6.4 %collective-permute-start.2 = (bf16[32,384]{1,0:T(8,128)(2,1)S(1)}, bf16[32,384]{1,0:T(8,128)(2,1)S(1)}, u32[]{:S(2)}, u32[]{:S(2)}) collective-permute-start(bf16[32,384]{1,0:T(8,128)(2,1)S(1)} %get-tuple-element.4), channel_id=1, source_target_pairs={{1,0},{2,1},{3,2},{4,3},{5,4},{6,5},{7,6},{9,8},{10,9},{11,10},{12... | collective-permute-start | bytes 73736 | tf_op jit(solution)/shard_map/ppermute | solution.py:17
  198.5 4.1 %collective-permute-start.3 = (bf16[32,384]{1,0:T(8,128)(2,1)S(1)}, bf16[32,384]{1,0:T(8,128)(2,1)S(1)}, u32[]{:S(2)}, u32[]{:S(2)}) collective-permute-start(bf16[32,384]{1,0:T(8,128)(2,1)S(1)} %get-tuple-element.5), channel_id=1, source_target_pairs={{0,1},{1,2},{2,3},{3,4},{4,5},{5,6},{6,7},{8,9},{9,10},{10,11},{11... | collective-permute-start | bytes 73736 | tf_op jit(solution)/shard_map/ppermute | solution.py:16
  202.5 1.4 copy-start.14
  203.6 72.6 %copy-start = (bf16[640,1536]{1,0:T(8,128)(2,1)S(1)}, bf16[640,1536]{1,0:T(8,128)(2,1)}, u32[]{:S(2)}) copy-start(bf16[640,1536]{1,0:T(8,128)(2,1)} %param.18) | copy-start | bytes 5898244
Sparse Core Ops, SparseCore 0:
  9.6 72.6 all-gather.4
  83.9 29.0 all-gather.6
  115.4 24.7 all-gather.8
  148.2 38.4 reduce-scatter.1
  194.2 81.9 all-reduce.2
where the time goes:
time: 287 us; the launch traced here: 286 us
  waiting for transfers between devices  198 us (69%)
  matrix products  29 us (10%)
  blocking collectives  17.5 us (6%)
  between operations  15.3 us (5%)
  other arithmetic  12.7 us (4%)
  starting transfers between devices  8.18 us (3%)
  local copies, waits for them, and re-layouts  5.62 us (2%)
    psum x1, waiting for transfers between devices, per_device(): d_head = lax.psum(spread.astype(jnp.bfloat16), 'batch').astype(jnp.float32)  68.3 us
    all_gather x1, waiting for transfers between devices, per_device(): lax.all_gather(dilated_weight, 'batch', axis=0, tiled=True)  44.9 us
    reduce_scatter x1, waiting for transfers between devices, per_device(): lax.psum_scatter(lax.dot_general(delta, embed, (((0,), (0,)), ((), ())),...  34.5 us
    all_gather x1, waiting for transfers between devices, per_device(): lax.all_gather(chosen, 'pos', axis=0, tiled=True)  24.8 us
    all_gather x1, waiting for transfers between devices, per_device(): lax.all_gather(w_point, 'batch', axis=0, tiled=True)  23.9 us
    unnamed x1, blocking collectives  17.5 us
  transfers between devices with their start and end apart: 9, of which 5 were waited for; matrix products, arithmetic and copies ran while one was open for 10% of the time, Pallas kernels for 0%

commit v1 on v0

--- a/solution.py
+++ b/solution.py
@@ -4,6 +4,18 @@
 from jax.sharding import PartitionSpec as P
 
 DILATION_STEP = 32
+
+
+def doubled_up(value, axis, dim):
+    ways, here, step = (lax.axis_size(axis), lax.axis_index(axis), value.shape[dim])
+    line, have = (value, 1)
+    while have < ways:
+        line = jnp.concatenate(
+            [line, lax.ppermute(line, axis, [(d, (d - have) % ways) for d in range(ways)])],
+            axis=dim,
+        )
+        have = 2 * have
+    return jnp.roll(line, here * step, axis=dim)
 
 
 def with_halo(shard, sides, width):
@@ -70,7 +82,7 @@
     chosen = head[slots]
     live_mark = (jnp.arange(slot_count) < assay_counts[0, 0]).astype(jnp.bfloat16)
     selected, live_all = (
-        lax.all_gather(chosen, "pos", axis=0, tiled=True),
+        doubled_up(chosen, "pos", 0),
         lax.all_gather(live_mark, "pos", axis=0, tiled=True),
     )
     pre = lax.dot_general(embed, selected, contract, preferred_element_type=jnp.float32)

time: 287 us -> 258 us (0.90)
  waiting for transfers between devices: 198 us -> 160 us
  starting transfers between devices: 8.18 us -> 14.1 us
  local copies, waits for them, and re-layouts: 5.62 us -> 11 us
    all_gather x1 -> x0, waiting for transfers between devices: 24.8 us -> none  [per_device(): lax.all_gather(chosen, 'pos', axis=0, tiled=True)]
    all_gather x1, waiting for transfers between devices: 44.9 us -> 27.4 us  [per_device(): lax.all_gather(dilated_weight, 'batch', axis=0, tiled=True)]
    unnamed x33 -> x40, local copies, waits for them, and re-layouts: 2.22 us -> 6.72 us
    ppermute x0 -> x3, starting transfers between devices: none -> 4.11 us  [doubled_up(): lax.ppermute(line, axis, [(d, (d - have) % ways) for d in range(ways)])]
    ppermute x0 -> x3, waiting for transfers between devices: none -> 4.03 us  [doubled_up(): lax.ppermute(line, axis, [(d, (d - have) % ways) for d in range(ways)])]
  transfers between devices with their start and end apart: 9 -> 11, of which waited for: 5 -> 8; matrix products, arithmetic and copies ran while one was open for 10% -> 13% of each run, Pallas kernels for 0% -> 0%
where the time goes in v1:
time: 258 us
  waiting for transfers between devices  160 us (62%)
  matrix products  27.6 us (11%)
  blocking collectives  15.3 us (6%)
  between operations  15.3 us (6%)
  other arithmetic  15 us (6%)
  starting transfers between devices  14.1 us (5%)
  local copies, waits for them, and re-layouts  11 us (4%)
    psum x1, waiting for transfers between devices, per_device(): d_head = lax.psum(spread.astype(jnp.bfloat16), 'batch').astype(jnp.float32)  69 us
    reduce_scatter x1, waiting for transfers between devices, per_device(): lax.psum_scatter(lax.dot_general(delta, embed, (((0,), (0,)), ((), ())),...  34.1 us
    all_gather x1, waiting for transfers between devices, per_device(): lax.all_gather(dilated_weight, 'batch', axis=0, tiled=True)  27.4 us
    all_gather x1, waiting for transfers between devices, per_device(): lax.all_gather(w_point, 'batch', axis=0, tiled=True)  23.3 us
    unnamed x1, blocking collectives  15.3 us
    ppermute x2, starting transfers between devices, with_halo(): before = lax.ppermute(last, axis, up)  7.27 us
    unnamed x40, local copies, waits for them, and re-layouts  6.72 us
  transfers between devices with their start and end apart: 11, of which 8 were waited for; matrix products, arithmetic and copies ran while one was open for 13% of the time, Pallas kernels for 0%

profile of v1, /device:TPU:0, one launch (start us, length us, event | category | flops | bytes accessed | tf_op | source)
XLA Modules:
  0.0 258.0 jit_solution(12469247922089281049)
XLA Ops:
  9.2 2.7 %gather_fusion = bf16[64,1536]{1,0:T(8,128)(2,1)S(1)} fusion(bf16[640,1536]{1,0:T(8,128)(2,1)} %param.18, s32[1024]{0:T(1024)S(1)} %pad_clamp_fusion), kind=kCustom, calls=%fused_computation | custom fusion | bytes 393472 | tf_op jit(solution)/shard_map/gather | solution.py:82
  11.9 3.4 %collective-permute-start.2 = (bf16[64,1536]{1,0:T(8,128)(2,1)S(1)}, bf16[64,1536]{1,0:T(8,128)(2,1)S(1)}, u32[]{:S(2)}, u32[]{:S(2)}) collective-permute-start(bf16[64,1536]{1,0:T(8,128)(2,1)S(1)} %gather_fusion), channel_id=1, source_target_pairs={{0,7},{1,0},{2,1},{3,2},{4,3},{5,4},{6,5},{7,6},{8,15},{9,8},{10,9... | collective-permute-start | bytes 589832 | tf_op jit(solution)/shard_map/ppermute | solution.py:14
  15.3 2.0 fusion.11
  17.3 1.2 collective-permute-done.2
  19.8 1.3 collective-permute-start.1
  21.1 5.5 %collective-permute-start = (bf16[32,1536]{1,0:T(8,128)(2,1)}, bf16[32,1536]{1,0:T(8,128)(2,1)}, u32[]{:S(2)}, u32[]{:S(2)}) collective-permute-start(bf16[32,1536]{1,0:T(8,128)(2,1)} %get-tuple-element.2), channel_id=1, source_target_pairs={{0,1},{1,2},{2,3},{3,4},{4,5},{5,6},{6,7},{8,9},{9,10},{10,11},{11... | collective-permute-start | bytes 294920 | tf_op jit(solution)/shard_map/ppermute | solution.py:28
  28.6 1.9 collective-permute-done.3
  31.7 15.3 %all-reduce = bf16[512]{0:T(512)(128)(2,1)S(1)} all-reduce(bf16[512]{0:T(512)(128)(2,1)S(1)} %dynamic-update-slice), channel_id=1, replica_groups=mesh['batch'=4,'pos'=8] {'pos'}, use_global_device_ids=true, to_apply=%add | all-reduce | flops 512 | bytes 2048
  49.8 1.0 collective-permute-done.4
  50.8 1.0 constant_dynamic-update-slice_fusion.4
  53.9 1.0 constant_dynamic-update-slice_fusion
  54.9 27.4 %all-gather.3.cloned.1.call-done = bf16[1536,3,384]{2,0,1:T(8,128)(2,1)} async-done(((bf16[384,3,384]{2,0,1:T(8,128)(2,1)}), bf16[1536,3,384]{2,0,1:T(8,128)(2,1)}) %all-gather.3.cloned.1.call-update) | async-done | bytes 3538960 | tf_op jit(solution)/shard_map/all_gather | solution.py:53
  82.3 3.3 %fusion.36 = f32[512,384]{1,0:T(8,128)S(1)} fusion(bf16[1,512,1536]{2,1,0:T(8,128)(2,1)} %param.11, f32[1536]{0:T(1024)S(1)} %copy-done.5, f32[1536]{0:T(1024)S(1)} %copy-done.6, bf16[1536,3,384]{2,0,1:T(8,128)(2,1)} %all-gather.3.cloned.1.call-done), kind=kOutput, calls=%fused_computation.51 | convolution fusion | flops 613416960 | bytes 3551232 | tf_op jit(solution)/shard_map/dot_general | solution.py:65
  85.6 1.0 fusion.32
  86.7 2.9 %fusion.45 = f32[512,384]{1,0:T(8,128)} fusion(f32[512,384]{1,0:T(8,128)S(1)} %fusion.32, f32[512,384]{1,0:T(8,128)S(1)} %fusion.36, bf16[512,1536]{1,0:T(8,128)(2,1)S(1)} %fusion.11, bf16[32,1536]{1,0:T(8,128)(2,1)} %collective-permute-done, bf16[1536,3,384]{2,0,1:T(8,128)(2,1)S(1)} %copy-done.3, f32[384]{0:T(512)S(1)} %copy-done.11, f32[384]{0:T(512)S(1)} %copy-done.12), kind=kOutput, calls=%fused_computation.60 | convolution fusion | flops 607911936 | bytes 5214208 | tf_op jit(solution)/shard_map/dot_general | solution.py:62
  89.6 23.3 %all-gather.5.cloned.1.call-done = bf16[384,1536]{1,0:T(8,128)(2,1)} async-done(((bf16[96,1536]{1,0:T(8,128)(2,1)}), bf16[384,1536]{1,0:T(8,128)(2,1)}) %all-gather.5.cloned.1.call-update) | async-done | bytes 1179664 | tf_op jit(solution)/shard_map/all_gather | solution.py:54
  112.9 2.5 fusion.27
  115.5 3.1 %fusion.50 = bf16[512,512]{1,0:T(8,128)(2,1)S(1)} fusion(bf16[512,1536]{1,0:T(8,128)(2,1)S(1)} %fusion.27, bf16[1024,1536]{1,0:T(8,128)(2,1)} %constant_dynamic-update-slice_fusion, s32[]{:T(128)S(6)} %select_n.30, bf16[1,512,512]{2,1,0:T(8,128)(2,1)S(1)} %copy-done.10, f32[512]{0:T(512)S(1)} %copy-done.7), kind=kOutput, calls=%fused_computation.70 | convolution fusion | flops 808976384 | bytes 4196356 | tf_op jit(solution)/shard_map/dot_general | solution.py:88
  118.6 2.1 convolution_convert_fusion
  120.8 3.5 %convolution_convert_fusion.1 = bf16[512,1536]{1,0:T(8,128)(2,1)} fusion(bf16[512,512]{1,0:T(8,128)(2,1)S(1)} %fusion.50, bf16[1024,1536]{1,0:T(8,128)(2,1)} %constant_dynamic-update-slice_fusion, s32[]{:T(128)S(6)} %select_n.30), kind=kOutput, calls=%fused_computation.39 | convolution fusion | flops 806092800 | bytes 3670020 | tf_op jit(solution)/shard_map/dot_general | solution.py:93
  124.4 34.1 %reduce-scatter.2.cloned.1.call-done = bf16[64,1536]{1,0:T(8,128)(2,1)} async-done(((bf16[512,1536]{1,0:T(8,128)(2,1)}), bf16[64,1536]{1,0:T(8,128)(2,1)}) %reduce-scatter.2.cloned.1.call-update) | async-done | bytes 196624 | tf_op jit(solution)/shard_map/reduce_scatter | solution.py:113
  158.5 3.7 %scatter_custom_fusion = f32[640,1536]{1,0:T(8,128)} fusion(s32[64]{0:T(128)} %copy-done.8, f32[]{:T(128)} %constant.52.clone.1, bf16[64,1536]{1,0:T(8,128)(2,1)} %reduce-scatter.2.cloned.1.call-done), kind=kCustom, calls=%fused_computation.42 | custom fusion | flops 196608 | bytes 4129280 | tf_op jit(solution)/shard_map/scatter-add | solution.py:121
  162.2 3.7 %convert_element_type.89 = bf16[640,1536]{1,0:T(8,128)(2,1)} convert(f32[640,1536]{1,0:T(8,128)} %scatter_custom_fusion) | non-fusion elementwise | flops 983040 | bytes 5898240 | tf_op jit(solution)/shard_map/convert_element_type | solution.py:122
  166.0 3.0 %fusion.46 = bf16[512,384]{1,0:T(8,128)(2,1)S(1)} fusion(bf16[512,1536]{1,0:T(8,128)(2,1)} %convolution_convert_fusion.1, bf16[384,1536]{1,0:T(8,128)(2,1)S(1)} %copy-done.9, f32[512,384]{1,0:T(8,128)} %fusion.45, f32[384]{0:T(512)S(1)} %copy-done.12), kind=kOutput, calls=%fused_computation.61 | convolution fusion | flops 607715328 | bytes 3933696 | tf_op jit(solution)/shard_map/dot_general | solution.py:94
  169.0 1.7 collective-permute-start.6
  170.7 1.3 collective-permute-start.5
  172.0 1.0 fusion.51
  173.1 1.0 fusion.52
  174.1 1.0 collective-permute-done.5
  175.1 4.0 %fusion.28 = bf16[1,512,1536]{2,1,0:T(8,128)(2,1)} fusion(bf16[1,512,1536]{2,1,0:T(8,128)(2,1)S(1)} %copy-done.2, f32[512,1536]{1,0:T(8,128)S(1)} %fusion.52, f32[512,1536]{1,0:T(8,128)S(1)} %fusion.51, bf16[512,1536]{1,0:T(8,128)(2,1)S(1)} %copy-done.14, f32[1536]{0:T(1024)S(1)} %copy-done.5, f32[1536]{0:T(1024)S(1)} %copy-done.6, ...), kind=kOutput, calls=%fused_computation.41 | convolution fusion | flops 625213440 | bytes 12623872 | tf_op jit(solution)/shard_map/dot_general | solution.py:97
  179.0 69.0 %all-reduce.3.cloned.1.call-done = bf16[640,1536]{1,0:T(8,128)(2,1)} async-done(((bf16[640,1536]{1,0:T(8,128)(2,1)}), bf16[640,1536]{1,0:T(8,128)(2,1)}) %all-reduce.3.cloned.1.call-update) | async-done | bytes 1966096 | tf_op jit(solution)/shard_map/psum | solution.py:122
  248.0 3.4 %subtract_convert_fusion = bf16[640,1536]{1,0:T(8,128)(2,1)} fusion(bf16[640,1536]{1,0:T(8,128)(2,1)} %all-reduce.3.cloned.1.call-done, bf16[640,1536]{1,0:T(8,128)(2,1)S(1)} %copy-done), kind=kLoop, calls=%fused_computation.9 | loop fusion | flops 4915200 | bytes 5898240 | tf_op jit(solution)/shard_map/convert_element_type | solution.py:123
  (60 shorter events, 10.3 us)
Async XLA Ops:
  7.2 8.1 %copy-start.1 = (bf16[1,512,1536]{2,1,0:T(8,128)(2,1)S(1)}, bf16[1,512,1536]{2,1,0:T(8,128)(2,1)}, u32[]{:S(2)}) copy-start(bf16[1,512,1536]{2,1,0:T(8,128)(2,1)} %param.11) | copy-start | bytes 4718596
  7.2 75.1 %all-gather.3.cloned.1.call-start = ((), (), s32[]{:S(2)}) async-start(), calls=%async_computation.1 | async-start | bytes 4423680 | tf_op jit(solution)/shard_map/all_gather | solution.py:53
  7.9 105.0 %all-gather.5.cloned.1.call-start = ((), (), s32[]{:S(2)}) async-start(), calls=%async_computation.2 | async-start | bytes 1474560 | tf_op jit(solution)/shard_map/all_gather | solution.py:54
  8.6 0.6 copy-start.8
  9.2 18.2 %copy-start.13 = (u32[32]{0:T(128)S(1)}, u32[32]{0:T(128)}, u32[]{:S(2)}) copy-start(u32[32]{0:T(128)} %constant.61) | copy-start | bytes 388
  11.9 6.6 %collective-permute-start.2 = (bf16[64,1536]{1,0:T(8,128)(2,1)S(1)}, bf16[64,1536]{1,0:T(8,128)(2,1)S(1)}, u32[]{:S(2)}, u32[]{:S(2)}) collective-permute-start(bf16[64,1536]{1,0:T(8,128)(2,1)S(1)} %gather_fusion), channel_id=1, source_target_pairs={{0,7},{1,0},{2,1},{3,2},{4,3},{5,4},{6,5},{7,6},{8,15},{9,8},{10,9... | collective-permute-start | bytes 589832 | tf_op jit(solution)/shard_map/ppermute | solution.py:14
  18.5 12.0 %collective-permute-start.3 = (bf16[128,1536]{1,0:T(8,128)(2,1)S(1)}, bf16[128,1536]{1,0:T(8,128)(2,1)S(1)}, u32[]{:S(2)}, u32[]{:S(2)}) collective-permute-start(bf16[128,1536]{1,0:T(8,128)(2,1)S(1)} %pad_maximum_fusion.17), channel_id=1, source_target_pairs={{0,6},{1,7},{2,0},{3,1},{4,2},{5,3},{6,4},{7,5},{8,14},{9,15},{10,... | collective-permute-start | bytes 1179656 | tf_op jit(solution)/shard_map/ppermute | solution.py:14
  19.8 65.8 %collective-permute-start.1 = (bf16[32,1536]{1,0:T(8,128)(2,1)S(1)}, bf16[32,1536]{1,0:T(8,128)(2,1)S(1)}, u32[]{:S(2)}, u32[]{:S(2)}) collective-permute-start(bf16[32,1536]{1,0:T(8,128)(2,1)S(1)} %get-tuple-element.3), channel_id=1, source_target_pairs={{1,0},{2,1},{3,2},{4,3},{5,4},{6,5},{7,6},{9,8},{10,9},{11,10},{12... | collective-permute-start | bytes 294920 | tf_op jit(solution)/shard_map/ppermute | solution.py:29
  21.1 65.6 %collective-permute-start = (bf16[32,1536]{1,0:T(8,128)(2,1)}, bf16[32,1536]{1,0:T(8,128)(2,1)}, u32[]{:S(2)}, u32[]{:S(2)}) collective-permute-start(bf16[32,1536]{1,0:T(8,128)(2,1)} %get-tuple-element.2), channel_id=1, source_target_pairs={{0,1},{1,2},{2,3},{3,4},{4,5},{5,6},{6,7},{8,9},{9,10},{10,11},{11... | collective-permute-start | bytes 294920 | tf_op jit(solution)/shard_map/ppermute | solution.py:28
  26.6 131.9 %reduce-scatter.2.cloned.1.call-start = ((), (), s32[]{:S(2)}) async-start(), calls=%async_computation.3 | async-start | bytes 1769472 | tf_op jit(solution)/shard_map/reduce_scatter | solution.py:113
  31.4 19.4 %collective-permute-start.4 = (bf16[256,1536]{1,0:T(8,128)(2,1)}, bf16[256,1536]{1,0:T(8,128)(2,1)S(1)}, u32[]{:S(2)}, u32[]{:S(2)}) collective-permute-start(bf16[256,1536]{1,0:T(8,128)(2,1)} %pad_maximum_fusion.12), channel_id=1, source_target_pairs={{0,4},{1,5},{2,6},{3,7},{4,0},{5,1},{6,2},{7,3},{8,12},{9,13},{10,... | collective-permute-start | bytes 2359304 | tf_op jit(solution)/shard_map/ppermute | solution.py:14
  47.7 34.6 %copy-start.5 = (f32[1536]{0:T(1024)S(1)}, f32[1536]{0:T(1024)}, u32[]{:S(2)}) copy-start(f32[1536]{0:T(1024)} %param.13) | copy-start | bytes 18436
  47.7 34.6 %copy-start.6 = (f32[1536]{0:T(1024)S(1)}, f32[1536]{0:T(1024)}, u32[]{:S(2)}) copy-start(f32[1536]{0:T(1024)} %param.12) | copy-start | bytes 18436
  82.3 3.4 %copy-start.3 = (bf16[1536,3,384]{2,0,1:T(8,128)(2,1)S(1)}, bf16[1536,3,384]{2,0,1:T(8,128)(2,1)}, u32[]{:S(2)}) copy-start(bf16[1536,3,384]{2,0,1:T(8,128)(2,1)} %all-gather.3.cloned.1.call-done) | copy-start | bytes 10616836
  85.6 1.1 copy-start.11
  85.6 1.1 copy-start.12
  86.6 26.3 %copy-start.2 = (bf16[1,512,1536]{2,1,0:T(8,128)(2,1)S(1)}, bf16[1,512,1536]{2,1,0:T(8,128)(2,1)}, u32[]{:S(2)}) copy-start(bf16[1,512,1536]{2,1,0:T(8,128)(2,1)} %param.11) | copy-start | bytes 4718596
  89.6 25.9 %copy-start.7 = (f32[512]{0:T(512)S(1)}, f32[512]{0:T(512)}, u32[]{:S(2)}) copy-start(f32[512]{0:T(512)} %convert_element_type.70) | copy-start | bytes 6148
  89.6 25.9 %copy-start.10 = (bf16[1,512,512]{2,1,0:T(8,128)(2,1)S(1)}, bf16[1,512,512]{2,1,0:T(8,128)(2,1)}, u32[]{:S(2)}) copy-start(bf16[1,512,512]{2,1,0:T(8,128)(2,1)} %param.19) | copy-start | bytes 1572868
  120.8 127.2 %all-reduce.3.cloned.1.call-start = ((), (), s32[]{:S(2)}) async-start(), calls=%async_computation.4 | async-start | bytes 3932160 | tf_op jit(solution)/shard_map/psum | solution.py:122
  162.2 3.7 %copy-start.9 = (bf16[384,1536]{1,0:T(8,128)(2,1)S(1)}, bf16[384,1536]{1,0:T(8,128)(2,1)}, u32[]{:S(2)}) copy-start(bf16[384,1536]{1,0:T(8,128)(2,1)} %all-gather.5.cloned.1.call-done) | copy-start | bytes 3538948
  166.0 6.1 %copy-start.4 = (bf16[1536,3,384]{2,0,1:T(8,128)(2,1)S(1)}, bf16[1536,3,384]{2,0,1:T(8,128)(2,1)}, u32[]{:S(2)}) copy-start(bf16[1536,3,384]{2,0,1:T(8,128)(2,1)} %all-gather.3.cloned.1.call-done) | copy-start | bytes 10616836
  169.0 4.1 %collective-permute-start.6 = (bf16[32,384]{1,0:T(8,128)(2,1)S(1)}, bf16[32,384]{1,0:T(8,128)(2,1)S(1)}, u32[]{:S(2)}, u32[]{:S(2)}) collective-permute-start(bf16[32,384]{1,0:T(8,128)(2,1)S(1)} %get-tuple-element.5), channel_id=1, source_target_pairs={{0,1},{1,2},{2,3},{3,4},{4,5},{5,6},{6,7},{8,9},{9,10},{10,11},{11... | collective-permute-start | bytes 73736 | tf_op jit(solution)/shard_map/ppermute | solution.py:28
  170.7 4.3 %collective-permute-start.5 = (bf16[32,384]{1,0:T(8,128)(2,1)S(1)}, bf16[32,384]{1,0:T(8,128)(2,1)S(1)}, u32[]{:S(2)}, u32[]{:S(2)}) collective-permute-start(bf16[32,384]{1,0:T(8,128)(2,1)S(1)} %get-tuple-element.4), channel_id=1, source_target_pairs={{1,0},{2,1},{3,2},{4,3},{5,4},{6,5},{7,6},{9,8},{10,9},{11,10},{12... | collective-permute-start | bytes 73736 | tf_op jit(solution)/shard_map/ppermute | solution.py:29
  173.1 2.0 copy-start.14
  174.1 73.9 %copy-start = (bf16[640,1536]{1,0:T(8,128)(2,1)S(1)}, bf16[640,1536]{1,0:T(8,128)(2,1)}, u32[]{:S(2)}) copy-start(bf16[640,1536]{1,0:T(8,128)(2,1)} %param.18) | copy-start | bytes 5898244
Sparse Core Ops, SparseCore 0:
  9.6 72.6 all-gather.2
  83.8 29.0 all-gather.4
  120.9 37.5 reduce-scatter.1
  166.1 81.9 all-reduce.2
